TPU v7x, 32 devices: a whole 2x2x4 slice. The times are simulated.
32 devices in a mesh: site: 8 (over z, y), sector: 4 (over x, core).
Axes of the slice: x: 2, y: 2, z: 4, core: 2. Of those that a mesh axis runs over, the one named last changes fastest.
Arguments:
- top_blocks: bfloat16 [8, 32, 512, 512], P('site', 'sector'), may hold values from -0.06363961 to 0.06363961
- bottom_blocks: bfloat16 [8, 32, 512, 512], P('site', 'sector'), may hold values from -0.06363961 to 0.06363961
- row_tensor: bfloat16 [8, 32, 512, 128], P('site', 'sector'), may hold values from -0.25 to 0.25
- merge_owner: int32 [8, 32, 1], P('site', 'sector'), may hold values from 0 to 3; in each aligned block of 8 rows (0 to 7, 8 to 15, ..., all dimensions but the last counted through in order) at most 4 rows name the same one
- merge_sub: int32 [8, 32], P('site', 'sector'), may hold values from 0 to 1
Outputs:
- top_canonical: float32 [8, 8, 128, 512], P('site', 'sector')
- bottom_canonical: float32 [8, 8, 128, 512], P('site', 'sector')
Inputs may be any that keep to these rules, and one draw needn't show every extreme that they name: `merge_owner`: among the 8 blocks of one device, at most 4 name one owner, a bound that some block reaches.
All inputs are finite; a program needn't handle non-finite values.
Results may differ from a plain program's by a relative error of at most 0.0014.
Values may be sent and summed in bfloat16 or wider, within the bound.
A program may use at most 64 MiB of HBM per device.

v0:
```python
import jax
import jax.numpy as jnp
from jax import lax
from jax.sharding import PartitionSpec as P

PH = 4
BD = 128
SEC_DEV = 2


def shifted(value, axis, steps):
    count = lax.axis_size(axis)
    first, last = (max(0, -steps), min(count, count - steps))
    return lax.ppermute(value, axis, [(source, source + steps) for source in range(first, last)])


def advance(carried, merged):
    grown = jnp.einsum("ulm,upmr->uplr", carried, merged, precision=lax.Precision.HIGHEST)
    gram = jnp.einsum("upla,uplb->uab", grown, grown, precision=lax.Precision.HIGHEST)
    lower = jnp.linalg.cholesky(gram)
    upper = jnp.swapaxes(lower, 1, 2)
    factor = lax.rsqrt(jnp.mean(upper * upper, axis=(1, 2), keepdims=True) + 1e-06)
    return (grown, lower, upper * factor)


def finish(grown, lower):
    count = grown.shape[0]
    turned = jnp.transpose(grown, (0, 3, 1, 2)).reshape(count, BD, PH * BD)
    return lax.linalg.triangular_solve(lower, turned, left_side=True, lower=True)


def place_slots(absorbed, table):
    placed = jnp.einsum("sj,jkr->skr", table, absorbed, preferred_element_type=jnp.float32)
    return placed.astype(jnp.bfloat16)


def gather_sectors(received, selector):
    merged = jnp.einsum("us,skr->ukr", selector, received, preferred_element_type=jnp.float32)
    merged = merged.reshape(SEC_DEV, PH, BD, BD)
    return merged.at[:, 0].add(jnp.eye(BD, dtype=jnp.float32))


def local(top_blocks, bottom_blocks, row_tensor, merge_owner, merge_sub):
    owners = lax.axis_size("sector")
    nblocks = top_blocks.shape[1]
    capacity = max(2, 2 * nblocks // owners)
    weights = row_tensor[0]
    absorbed_top = jnp.einsum(
        "jkc,jcr->jkr", top_blocks[0], weights, preferred_element_type=jnp.float32
    ).astype(jnp.bfloat16)
    absorbed_bottom = jnp.einsum(
        "jkc,jcr->jkr", bottom_blocks[0], weights, preferred_element_type=jnp.float32
    ).astype(jnp.bfloat16)
    owner = merge_owner[0, :, 0]
    member = merge_sub[0]
    order = jnp.arange(nblocks, dtype=jnp.int32)
    alike = (owner[:, None] == owner[None, :]) & (order[None, :] < order[:, None])
    rank = jnp.sum(alike.astype(jnp.int32), axis=1)
    slot_id = owner * capacity + rank
    slots = jnp.arange(owners * capacity, dtype=jnp.int32)
    hits = slots[:, None] == slot_id[None, :]
    table = hits.astype(jnp.bfloat16)
    labels = jnp.sum(jnp.where(hits, member[None, :] + 1, 0), axis=1).astype(jnp.bfloat16)
    send_top = place_slots(absorbed_top, table).reshape(owners, capacity, PH * BD, BD)
    send_bottom = place_slots(absorbed_bottom, table).reshape(owners, capacity, PH * BD, BD)
    send_labels = labels.reshape(owners, capacity)
    recv_top, recv_bottom, recv_labels = (
        lax.all_to_all(send_top, "sector", split_axis=0, concat_axis=0, tiled=True),
        lax.all_to_all(send_bottom, "sector", split_axis=0, concat_axis=0, tiled=True),
        lax.all_to_all(send_labels, "sector", split_axis=0, concat_axis=0, tiled=True),
    )
    flat_labels = recv_labels.reshape(owners * capacity).astype(jnp.float32)
    wanted = jnp.arange(1, SEC_DEV + 1, dtype=jnp.float32)
    selector = (flat_labels[None, :] == wanted[:, None]).astype(jnp.bfloat16)
    merged_top = gather_sectors(recv_top.reshape(owners * capacity, PH * BD, BD), selector)
    merged_bottom = gather_sectors(recv_bottom.reshape(owners * capacity, PH * BD, BD), selector)
    first = lax.axis_index("site") == 0
    identity = jnp.broadcast_to(jnp.eye(BD, dtype=jnp.float32), (SEC_DEV, BD, BD))
    turns = lax.axis_size("site") - 1

    def pair_step(step, carried):
        unused_a, unused_b, next_top = advance(carried[0], merged_top)
        moved_top = shifted(next_top, "site", 1)
        unused_c, unused_d, next_bottom = advance(carried[1], merged_bottom)
        moved_bottom = shifted(next_bottom, "site", 1)
        return (jnp.where(first, identity, moved_top), jnp.where(first, identity, moved_bottom))

    carried_top, carried_bottom = lax.fori_loop(0, turns, pair_step, (identity, identity))
    grown_top, lower_top, unused_e = advance(carried_top, merged_top)
    grown_bottom, lower_bottom, unused_f = advance(carried_bottom, merged_bottom)
    top_canonical = finish(grown_top, lower_top)[None]
    bottom_canonical = finish(grown_bottom, lower_bottom)[None]
    return (top_canonical, bottom_canonical)


def solution(mesh):
    placed = (
        P("site", "sector", None, None),
        P("site", "sector", None, None),
        P("site", "sector", None, None),
        P("site", "sector", None),
        P("site", "sector"),
    )
    return jax.shard_map(
        local,
        mesh=mesh,
        in_specs=placed,
        out_specs=(P("site", "sector", None, None), P("site", "sector", None, None)),
        check_vma=False,
    )
```

profile of v0, /device:TPU:0, one launch (start us, length us, event | category | flops | bytes accessed | tf_op | source)
XLA Modules:
  0.0 600.9 jit_solution(205283555628860070)
XLA Ops:
  0.6 0.9 convert_reduce_fusion
  1.6 0.7 multiply_add_fusion
  2.2 0.7 add_bitcast_fusion
  3.0 0.7 convert_element_type.67
  3.7 4.2 all-to-all-start
  7.9 3.4 fusion.10
  11.3 1.0 convolution_convert_fusion.1
  12.3 2.0 copy.86
  14.4 3.6 all-to-all-start.1
  18.0 3.4 fusion.13
  21.4 1.0 convolution_convert_fusion
  22.4 2.1 copy.91
  24.5 19.1 %all-to-all-done.1 = bf16[4,4,512,128]{3,1,2,0:T(4,128)(2,1)S(1)} async-done(((bf16[4,4,512,128]{3,1,2,0:T(4,128)(2,1)}), bf16[4,4,512,128]{3,1,2,0:T(4,128)(2,1)S(1)}, u32[]{:S(2)}, u32[]{:S(2)}) %all-to-all-start.1) | async-done | bytes 2097184 | tf_op jit(solution)/shard_map/all_to_all | solution.py:68
  43.6 4.4 all-to-all-start.2
  48.8 1.4 copy.88
  50.2 23.7 %all-to-all-done.2 = bf16[4,4,512,128]{3,1,2,0:T(4,128)(2,1)} async-done(((bf16[4,4,512,128]{3,1,2,0:T(4,128)(2,1)}), bf16[4,4,512,128]{3,1,2,0:T(4,128)(2,1)}, u32[]{:S(2)}, u32[]{:S(2)}) %all-to-all-start.2) | async-done | bytes 2097184 | tf_op jit(solution)/shard_map/all_to_all | solution.py:69
  73.9 2.0 copy.92
  75.9 1.4 copy.93
  78.4 0.8 copy-done.1
  79.1 1.2 copy.94
  80.6 426.6 %while.16 = (s32[]{:T(128)}, f32[2,128,128]{1,2,0:T(8,128)S(1)}, f32[2,128,128]{1,2,0:T(8,128)S(1)}, pred[]{:T(512)}, f32[2,4,128,128]{2,3,1,0:T(8,128)S(1)}, /*...) while((s32[]{:T(128)}, f32[2,128,128]{1,2,0:T(8,128)S(1)}, ...), condition=%wide.region_7.9_spmd.clone.clone, body=%wide.region_2.8_spmd.clone.clone.sunk | while | flops 806126080 | bytes 7753970 | solution.py:88
  82.2 23.5 %custom-call.19 = f32[2,128,128]{2,1,0:T(8,128)S(1)} custom-call(f32[2,128,128]{2,1,0:T(8,128)S(1)} %fusion.80), custom_call_target="Cholesky" | custom-call | tf_op jit(solution)/shard_map/while/body/eval_jaxpr/jit(cholesky)/cholesky | solution.py:20
  107.0 23.5 %custom-call.18 = f32[2,128,128]{2,1,0:T(8,128)S(1)} custom-call(f32[2,128,128]{2,1,0:T(8,128)S(1)} %fusion.79), custom_call_target="Cholesky" | custom-call | tf_op jit(solution)/shard_map/while/body/eval_jaxpr/jit(cholesky)/cholesky | solution.py:20
  131.0 3.9 collective-permute-start
  134.9 3.4 collective-permute-start.1
  138.4 2.5 collective-permute-done.1
  142.3 23.5 %custom-call.19 = f32[2,128,128]{2,1,0:T(8,128)S(1)} custom-call(f32[2,128,128]{2,1,0:T(8,128)S(1)} %fusion.80), custom_call_target="Cholesky" | custom-call | tf_op jit(solution)/shard_map/while/body/eval_jaxpr/jit(cholesky)/cholesky | solution.py:20
  167.1 23.5 %custom-call.18 = f32[2,128,128]{2,1,0:T(8,128)S(1)} custom-call(f32[2,128,128]{2,1,0:T(8,128)S(1)} %fusion.79), custom_call_target="Cholesky" | custom-call | tf_op jit(solution)/shard_map/while/body/eval_jaxpr/jit(cholesky)/cholesky | solution.py:20
  191.1 4.4 collective-permute-start
  195.5 4.3 collective-permute-start.1
  199.8 2.5 collective-permute-done.1
  203.7 23.5 %custom-call.19 = f32[2,128,128]{2,1,0:T(8,128)S(1)} custom-call(f32[2,128,128]{2,1,0:T(8,128)S(1)} %fusion.80), custom_call_target="Cholesky" | custom-call | tf_op jit(solution)/shard_map/while/body/eval_jaxpr/jit(cholesky)/cholesky | solution.py:20
  228.5 23.5 %custom-call.18 = f32[2,128,128]{2,1,0:T(8,128)S(1)} custom-call(f32[2,128,128]{2,1,0:T(8,128)S(1)} %fusion.79), custom_call_target="Cholesky" | custom-call | tf_op jit(solution)/shard_map/while/body/eval_jaxpr/jit(cholesky)/cholesky | solution.py:20
  252.5 4.4 collective-permute-start
  256.9 3.4 collective-permute-start.1
  260.5 2.3 collective-permute-done.1
  264.3 23.5 %custom-call.19 = f32[2,128,128]{2,1,0:T(8,128)S(1)} custom-call(f32[2,128,128]{2,1,0:T(8,128)S(1)} %fusion.80), custom_call_target="Cholesky" | custom-call | tf_op jit(solution)/shard_map/while/body/eval_jaxpr/jit(cholesky)/cholesky | solution.py:20
  289.1 23.5 %custom-call.18 = f32[2,128,128]{2,1,0:T(8,128)S(1)} custom-call(f32[2,128,128]{2,1,0:T(8,128)S(1)} %fusion.79), custom_call_target="Cholesky" | custom-call | tf_op jit(solution)/shard_map/while/body/eval_jaxpr/jit(cholesky)/cholesky | solution.py:20
  313.1 4.4 collective-permute-start
  317.4 4.3 collective-permute-start.1
  321.8 2.5 collective-permute-done.1
  325.7 23.5 %custom-call.19 = f32[2,128,128]{2,1,0:T(8,128)S(1)} custom-call(f32[2,128,128]{2,1,0:T(8,128)S(1)} %fusion.80), custom_call_target="Cholesky" | custom-call | tf_op jit(solution)/shard_map/while/body/eval_jaxpr/jit(cholesky)/cholesky | solution.py:20
  350.5 23.5 %custom-call.18 = f32[2,128,128]{2,1,0:T(8,128)S(1)} custom-call(f32[2,128,128]{2,1,0:T(8,128)S(1)} %fusion.79), custom_call_target="Cholesky" | custom-call | tf_op jit(solution)/shard_map/while/body/eval_jaxpr/jit(cholesky)/cholesky | solution.py:20
  374.5 4.4 collective-permute-start
  378.9 3.4 collective-permute-start.1
  382.3 2.5 collective-permute-done.1
  386.3 23.5 %custom-call.19 = f32[2,128,128]{2,1,0:T(8,128)S(1)} custom-call(f32[2,128,128]{2,1,0:T(8,128)S(1)} %fusion.80), custom_call_target="Cholesky" | custom-call | tf_op jit(solution)/shard_map/while/body/eval_jaxpr/jit(cholesky)/cholesky | solution.py:20
  411.1 23.5 %custom-call.18 = f32[2,128,128]{2,1,0:T(8,128)S(1)} custom-call(f32[2,128,128]{2,1,0:T(8,128)S(1)} %fusion.79), custom_call_target="Cholesky" | custom-call | tf_op jit(solution)/shard_map/while/body/eval_jaxpr/jit(cholesky)/cholesky | solution.py:20
  435.1 4.4 collective-permute-start
  439.4 4.3 collective-permute-start.1
  443.8 2.5 collective-permute-done.1
  447.7 23.5 %custom-call.19 = f32[2,128,128]{2,1,0:T(8,128)S(1)} custom-call(f32[2,128,128]{2,1,0:T(8,128)S(1)} %fusion.80), custom_call_target="Cholesky" | custom-call | tf_op jit(solution)/shard_map/while/body/eval_jaxpr/jit(cholesky)/cholesky | solution.py:20
  472.5 23.5 %custom-call.18 = f32[2,128,128]{2,1,0:T(8,128)S(1)} custom-call(f32[2,128,128]{2,1,0:T(8,128)S(1)} %fusion.79), custom_call_target="Cholesky" | custom-call | tf_op jit(solution)/shard_map/while/body/eval_jaxpr/jit(cholesky)/cholesky | solution.py:20
  496.5 4.4 collective-permute-start
  500.8 3.6 collective-permute-start.1
  504.5 2.5 collective-permute-done.1
  507.8 1.0 convolution_bitcast_fusion.7
  509.0 23.5 %custom-call.12 = f32[2,128,128]{2,1,0:T(8,128)S(1)} custom-call(f32[2,128,128]{2,1,0:T(8,128)S(1)} %fusion.31), custom_call_target="Cholesky" | custom-call | tf_op jit(solution)/shard_map/jit(cholesky)/cholesky | solution.py:20
  533.1 1.0 convolution_bitcast_fusion.6
  534.2 23.5 %custom-call.14 = f32[2,128,128]{2,1,0:T(8,128)S(1)} custom-call(f32[2,128,128]{2,1,0:T(8,128)S(1)} %fusion.29), custom_call_target="Cholesky" | custom-call | tf_op jit(solution)/shard_map/jit(cholesky)/cholesky | solution.py:20
  558.0 19.9 %custom-call.15 = f32[2,1,128,128]{2,3,1,0:T(8,128)S(1)} custom-call(f32[2,1,128,128]{3,2,1,0:T(8,128)S(1)} %get-tuple-element.162), custom_call_target="InvertDiagBlocksLowerTriangular" | custom-call | tf_op jit(solution)/shard_map/triangular_solve/custom-call.0 | solution.py:29
  577.9 19.7 %custom-call.13 = f32[2,1,128,128]{2,3,1,0:T(8,128)S(1)} custom-call(f32[2,1,128,128]{3,2,1,0:T(8,128)S(1)} %get-tuple-element.163), custom_call_target="InvertDiagBlocksLowerTriangular" | custom-call | tf_op jit(solution)/shard_map/triangular_solve/custom-call.0 | solution.py:29
  597.6 1.4 convolution_bitcast_fusion.4
  599.0 1.4 convolution_bitcast_fusion.5
  (155 shorter events, 26.6 us)
Async XLA Ops:
  0.6 7.2 %copy-start = (bf16[1,8,512,128]{3,2,1,0:T(8,128)(2,1)S(1)}, bf16[1,8,512,128]{3,2,1,0:T(8,128)(2,1)}, u32[]{:S(2)}) copy-start(bf16[1,8,512,128]{3,2,1,0:T(8,128)(2,1)} %param.16) | copy-start | bytes 3145732
  3.7 10.7 %all-to-all-start = ((bf16[4,1,4]{2,1,0:T(2,128)(2,1)}), bf16[4,1,4]{2,1,0:T(2,128)(2,1)S(1)}, u32[]{:S(2)}, u32[]{:S(2)}) async-start(bf16[4,1,4]{2,1,0:T(2,128)(2,1)} %convert_element_type.67), calls=%async_computation | async-start | bytes 4096 | tf_op jit(solution)/shard_map/all_to_all | solution.py:70
  14.4 29.3 %all-to-all-start.1 = ((bf16[4,4,512,128]{3,1,2,0:T(4,128)(2,1)}), bf16[4,4,512,128]{3,1,2,0:T(4,128)(2,1)S(1)}, u32[]{:S(2)}, u32[]{:S(2)}) async-start(bf16[4,4,512,128]{3,1,2,0:T(4,128)(2,1)} %copy.86), calls=%async_computation.1 | async-start | bytes 4194304 | tf_op jit(solution)/shard_map/all_to_all | solution.py:68
  43.6 30.2 %all-to-all-start.2 = ((bf16[4,4,512,128]{3,1,2,0:T(4,128)(2,1)}), bf16[4,4,512,128]{3,1,2,0:T(4,128)(2,1)}, u32[]{:S(2)}, u32[]{:S(2)}) async-start(bf16[4,4,512,128]{3,1,2,0:T(4,128)(2,1)} %copy.91), calls=%async_computation.2 | async-start | bytes 4194304 | tf_op jit(solution)/shard_map/all_to_all | solution.py:69
  78.3 0.8 copy-start.1
  131.0 7.4 %collective-permute-start = (f32[2,128,128]{1,2,0:T(8,128)S(1)}, f32[2,128,128]{1,2,0:T(8,128)S(1)}, u32[]{:S(2)}, u32[]{:S(2)}) collective-permute-start(f32[2,128,128]{1,2,0:T(8,128)S(1)} %get-tuple-element.225), channel_id=1, source_target_pairs={{0,4},{4,8},{8,12},{12,16},{16,20},{20,24},{24,28},{1,5},{5,9},{9,... | collective-permute-start | bytes 393224 | tf_op jit(solution)/shard_map/while/body/eval_jaxpr/ppermute | solution.py:14
  134.9 5.9 collective-permute-start.1
  191.1 8.7 %collective-permute-start = (f32[2,128,128]{1,2,0:T(8,128)S(1)}, f32[2,128,128]{1,2,0:T(8,128)S(1)}, u32[]{:S(2)}, u32[]{:S(2)}) collective-permute-start(f32[2,128,128]{1,2,0:T(8,128)S(1)} %get-tuple-element.225), channel_id=1, source_target_pairs={{0,4},{4,8},{8,12},{12,16},{16,20},{20,24},{24,28},{1,5},{5,9},{9,... | collective-permute-start | bytes 393224 | tf_op jit(solution)/shard_map/while/body/eval_jaxpr/ppermute | solution.py:14
  195.5 6.8 %collective-permute-start.1 = (f32[2,128,128]{1,2,0:T(8,128)S(1)}, f32[2,128,128]{1,2,0:T(8,128)S(1)}, u32[]{:S(2)}, u32[]{:S(2)}) collective-permute-start(f32[2,128,128]{1,2,0:T(8,128)S(1)} %get-tuple-element.226), channel_id=1, source_target_pairs={{0,4},{4,8},{8,12},{12,16},{16,20},{20,24},{24,28},{1,5},{5,9},{9,... | collective-permute-start | bytes 393224 | tf_op jit(solution)/shard_map/while/body/eval_jaxpr/ppermute | solution.py:14
  252.5 8.0 %collective-permute-start = (f32[2,128,128]{1,2,0:T(8,128)S(1)}, f32[2,128,128]{1,2,0:T(8,128)S(1)}, u32[]{:S(2)}, u32[]{:S(2)}) collective-permute-start(f32[2,128,128]{1,2,0:T(8,128)S(1)} %get-tuple-element.225), channel_id=1, source_target_pairs={{0,4},{4,8},{8,12},{12,16},{16,20},{20,24},{24,28},{1,5},{5,9},{9,... | collective-permute-start | bytes 393224 | tf_op jit(solution)/shard_map/while/body/eval_jaxpr/ppermute | solution.py:14
  256.9 5.9 collective-permute-start.1
  313.1 8.7 %collective-permute-start = (f32[2,128,128]{1,2,0:T(8,128)S(1)}, f32[2,128,128]{1,2,0:T(8,128)S(1)}, u32[]{:S(2)}, u32[]{:S(2)}) collective-permute-start(f32[2,128,128]{1,2,0:T(8,128)S(1)} %get-tuple-element.225), channel_id=1, source_target_pairs={{0,4},{4,8},{8,12},{12,16},{16,20},{20,24},{24,28},{1,5},{5,9},{9,... | collective-permute-start | bytes 393224 | tf_op jit(solution)/shard_map/while/body/eval_jaxpr/ppermute | solution.py:14
  317.4 6.8 %collective-permute-start.1 = (f32[2,128,128]{1,2,0:T(8,128)S(1)}, f32[2,128,128]{1,2,0:T(8,128)S(1)}, u32[]{:S(2)}, u32[]{:S(2)}) collective-permute-start(f32[2,128,128]{1,2,0:T(8,128)S(1)} %get-tuple-element.226), channel_id=1, source_target_pairs={{0,4},{4,8},{8,12},{12,16},{16,20},{20,24},{24,28},{1,5},{5,9},{9,... | collective-permute-start | bytes 393224 | tf_op jit(solution)/shard_map/while/body/eval_jaxpr/ppermute | solution.py:14
  374.5 7.8 %collective-permute-start = (f32[2,128,128]{1,2,0:T(8,128)S(1)}, f32[2,128,128]{1,2,0:T(8,128)S(1)}, u32[]{:S(2)}, u32[]{:S(2)}) collective-permute-start(f32[2,128,128]{1,2,0:T(8,128)S(1)} %get-tuple-element.225), channel_id=1, source_target_pairs={{0,4},{4,8},{8,12},{12,16},{16,20},{20,24},{24,28},{1,5},{5,9},{9,... | collective-permute-start | bytes 393224 | tf_op jit(solution)/shard_map/while/body/eval_jaxpr/ppermute | solution.py:14
  378.9 6.0 collective-permute-start.1
  435.1 8.7 %collective-permute-start = (f32[2,128,128]{1,2,0:T(8,128)S(1)}, f32[2,128,128]{1,2,0:T(8,128)S(1)}, u32[]{:S(2)}, u32[]{:S(2)}) collective-permute-start(f32[2,128,128]{1,2,0:T(8,128)S(1)} %get-tuple-element.225), channel_id=1, source_target_pairs={{0,4},{4,8},{8,12},{12,16},{16,20},{20,24},{24,28},{1,5},{5,9},{9,... | collective-permute-start | bytes 393224 | tf_op jit(solution)/shard_map/while/body/eval_jaxpr/ppermute | solution.py:14
  439.4 6.8 %collective-permute-start.1 = (f32[2,128,128]{1,2,0:T(8,128)S(1)}, f32[2,128,128]{1,2,0:T(8,128)S(1)}, u32[]{:S(2)}, u32[]{:S(2)}) collective-permute-start(f32[2,128,128]{1,2,0:T(8,128)S(1)} %get-tuple-element.226), channel_id=1, source_target_pairs={{0,4},{4,8},{8,12},{12,16},{16,20},{20,24},{24,28},{1,5},{5,9},{9,... | collective-permute-start | bytes 393224 | tf_op jit(solution)/shard_map/while/body/eval_jaxpr/ppermute | solution.py:14
  496.5 8.0 %collective-permute-start = (f32[2,128,128]{1,2,0:T(8,128)S(1)}, f32[2,128,128]{1,2,0:T(8,128)S(1)}, u32[]{:S(2)}, u32[]{:S(2)}) collective-permute-start(f32[2,128,128]{1,2,0:T(8,128)S(1)} %get-tuple-element.225), channel_id=1, source_target_pairs={{0,4},{4,8},{8,12},{12,16},{16,20},{20,24},{24,28},{1,5},{5,9},{9,... | collective-permute-start | bytes 393224 | tf_op jit(solution)/shard_map/while/body/eval_jaxpr/ppermute | solution.py:14
  500.8 6.1 %collective-permute-start.1 = (f32[2,128,128]{1,2,0:T(8,128)S(1)}, f32[2,128,128]{1,2,0:T(8,128)S(1)}, u32[]{:S(2)}, u32[]{:S(2)}) collective-permute-start(f32[2,128,128]{1,2,0:T(8,128)S(1)} %get-tuple-element.226), channel_id=1, source_target_pairs={{0,4},{4,8},{8,12},{12,16},{16,20},{20,24},{24,28},{1,5},{5,9},{9,... | collective-permute-start | bytes 393224 | tf_op jit(solution)/shard_map/while/body/eval_jaxpr/ppermute | solution.py:14
where the time goes:
time: 609 us; the launch traced here: 601 us
  other arithmetic  422 us (69%)
  starting transfers between devices  69.2 us (11%)
  waiting for transfers between devices  60.3 us (10%)
  matrix products  32.9 us (5%)
  local copies, waits for them, and re-layouts  13.8 us (2%)
    another operation x40, other arithmetic, advance(): lower = jnp.linalg.cholesky(gram)  377 us
    ppermute x14, starting transfers between devices, shifted(): lax.ppermute(value, axis, [(source, source + steps) for source in range(f...  56.9 us
    another operation x4, other arithmetic, finish(): lax.linalg.triangular_solve(lower, turned, left_side=True, lower=True)  39.7 us
    all_to_all x1, waiting for transfers between devices, local(): lax.all_to_all(send_bottom, 'sector', split_axis=0, concat_axis=0, tiled=...  23.7 us
    all_to_all x1, waiting for transfers between devices, local(): lax.all_to_all(send_top, 'sector', split_axis=0, concat_axis=0, tiled=True)  19.1 us
    ppermute x14, waiting for transfers between devices, shifted(): lax.ppermute(value, axis, [(source, source + steps) for source in range(f...  17.4 us
  transfers between devices with their start and end apart: 17, of which 10 were waited for; matrix products, arithmetic and copies ran while one was open for 2% of the time, Pallas kernels for 0%

commit v1 on v0

v1 whole, which is shorter than its diff:
```python
import functools

import jax
import jax.numpy as jnp
from jax import lax
from jax.experimental import pallas as pl
from jax.experimental.pallas import tpu as pltpu
from jax.sharding import PartitionSpec as P

PH = 4
BD = 128
SEC_DEV = 2
CHAINS = 4
PANEL = 32
WIDTH = 4
HIGHEST = lax.Precision.HIGHEST
NT = (((1,), (1,)), ((), ()))


def mm(a, b):
    return jnp.dot(a, b, precision=HIGHEST, preferred_element_type=jnp.float32)


def mm_nt(a, b):
    return lax.dot_general(a, b, NT, precision=HIGHEST, preferred_element_type=jnp.float32)


def mm_tn(a, b):
    return lax.dot_general(
        a, b, (((0,), (0,)), ((), ())), precision=HIGHEST, preferred_element_type=jnp.float32
    )


def absorb_kernel(target, top, bottom, weights, partial):
    step = pl.program_id(0)

    @pl.when(step == 0)
    def _():
        partial[...] = jnp.zeros_like(partial)

    sector = target[step]
    for boundary, blocks in enumerate((top, bottom)):
        absorbed = jnp.dot(blocks[0, 0], weights[0, 0], preferred_element_type=jnp.float32)
        partial[sector, boundary] += absorbed.astype(jnp.bfloat16).astype(jnp.float32)


def absorb(target, top_blocks, bottom_blocks, row_tensor, sectors):
    count, rows, inner = top_blocks.shape[1:]
    block = lambda *tail: pl.BlockSpec((1, 1) + tail, lambda j, t: (0, j, 0, 0))
    return pl.pallas_call(
        absorb_kernel,
        out_shape=jax.ShapeDtypeStruct((sectors, 2, rows, BD), jnp.float32),
        grid_spec=pltpu.PrefetchScalarGridSpec(
            num_scalar_prefetch=1,
            grid=(count,),
            in_specs=[block(rows, inner), block(rows, inner), block(inner, BD)],
            out_specs=pl.BlockSpec((sectors, 2, rows, BD), lambda j, t: (0, 0, 0, 0)),
        ),
        compiler_params=pltpu.CompilerParams(vmem_limit_bytes=48 * 2**20),
        name="absorb",
    )(target, top_blocks, bottom_blocks, row_tensor)


def identity():
    return (
        lax.broadcasted_iota(jnp.int32, (BD, BD), 0) == lax.broadcasted_iota(jnp.int32, (BD, BD), 1)
    ).astype(jnp.float32)


def sweep_kernel(
    sites, owners, partial, m_out, x_out, g_out,
    own, near, away, landed, leaving, arriving, turned,
    own_sem, near_send, near_recv, away_send, away_recv, site_send, site_recv,
):
    chips = owners // 2
    site = lax.axis_index("site")
    sector = lax.axis_index("sector")
    core = sector % 2
    chip = sector // 2

    def at(site_to, sector_to):
        return (site_to, sector_to)

    partner = at(site, chip * 2 + (1 - core))

    def mate(shift):
        return at(site, ((chip + shift) % chips) * 2 + core)

    barrier = pltpu.get_barrier_semaphore()
    for device in [partner] + [mate(shift) for shift in range(1, chips)]:
        pl.semaphore_signal(barrier, inc=1, device_id=device, device_id_type=pl.DeviceIdType.MESH)

    @pl.when(site > 0)
    def _():
        pl.semaphore_signal(
            barrier, inc=1, device_id=at(site - 1, sector), device_id_type=pl.DeviceIdType.MESH
        )

    @pl.when(site < sites - 1)
    def _():
        pl.semaphore_signal(
            barrier, inc=1, device_id=at(site + 1, sector), device_id_type=pl.DeviceIdType.MESH
        )

    sides = jnp.where(site > 0, 1, 0) + jnp.where(site < sites - 1, 1, 0)
    pl.semaphore_wait(barrier, chips + sides)

    def own_copy(shift, k):
        owner = ((chip + shift) % chips) * 2 + core
        return pltpu.make_async_copy(partial.at[owner, k], own.at[shift, k], own_sem.at[shift, k])

    def near_copy(shift, k):
        owner = ((chip + shift) % chips) * 2 + (1 - core)
        return pltpu.make_async_remote_copy(
            src_ref=partial.at[owner, k], dst_ref=near.at[shift, k],
            send_sem=near_send.at[shift, k], recv_sem=near_recv.at[shift, k],
            device_id=partner, device_id_type=pl.DeviceIdType.MESH,
        )

    def away_copy(shift, k):
        return pltpu.make_async_remote_copy(
            src_ref=away.at[shift - 1, k], dst_ref=landed.at[shift - 1, k],
            send_sem=away_send.at[shift - 1, k], recv_sem=away_recv.at[shift - 1, k],
            device_id=mate(shift), device_id_type=pl.DeviceIdType.MESH,
        )

    def site_copy(k):
        return pltpu.make_async_remote_copy(
            src_ref=leaving.at[k], dst_ref=arriving.at[k],
            send_sem=site_send.at[k], recv_sem=site_recv.at[k],
            device_id=at(site + 1, sector), device_id_type=pl.DeviceIdType.MESH,
        )

    order = list(range(1, chips)) + [0]
    for shift in order:
        @pl.loop(0, CHAINS)
        def _(k):
            near_copy(shift, k).start()
            own_copy(shift, k).start()

    @pl.loop(0, CHAINS)
    def _(k):
        for shift in range(1, chips):
            near_copy(shift, k).wait_recv()
            own_copy(shift, k).wait()
            away[shift - 1, k] = (near[shift, k] + own[shift, k]).astype(jnp.bfloat16)
            away_copy(shift, k).start()

    eye = identity()

    @pl.loop(0, CHAINS)
    def _(k):
        near_copy(0, k).wait_recv()
        own_copy(0, k).wait()
        for shift in range(1, chips):
            away_copy(shift, k).wait_recv()
        for p in range(PH):
            rows = pl.ds(p * BD, BD)
            merged = near[0, k, rows, :] + own[0, k, rows, :]
            for shift in range(1, chips):
                merged += landed[shift - 1, k, rows, :].astype(jnp.float32)
            if p == 0:
                merged += eye
            m_out[k, rows, :] = merged
            turned[rows, :] = merged.T

        @pl.when(site == 0)
        def _():
            x_out[k] = eye

        @pl.when(site > 0)
        def _():
            site_copy(k).wait_recv()
            x_out[k] = arriving[k]

        half = mm(turned[...], x_out[k])
        gram = mm(half[:BD], m_out[k, pl.ds(0, BD), :])
        for p in range(1, PH):
            gram += mm(half[p * BD:(p + 1) * BD], m_out[k, pl.ds(p * BD, BD), :])
        g_out[k] = gram

        @pl.when(site < sites - 1)
        def _():
            trace = jnp.sum(jnp.sum(gram * eye, axis=0, keepdims=True), axis=1, keepdims=True)
            leaving[k] = gram / (trace * (1.0 / (BD * BD)) + 1e-06)
            site_copy(k).start()

    @pl.loop(0, CHAINS)
    def _(k):
        for shift in range(chips):
            near_copy(shift, k).wait_send()
        for shift in range(1, chips):
            away_copy(shift, k).wait_send()

        @pl.when(site < sites - 1)
        def _():
            site_copy(k).wait_send()


def sweep(partial, sites, owners):
    chips = owners // 2
    rows = PH * BD
    vmem = pl.BlockSpec(memory_space=pltpu.VMEM)
    f32 = jnp.float32
    dma = pltpu.SemaphoreType.DMA
    return pl.pallas_call(
        functools.partial(sweep_kernel, sites, owners),
        out_shape=(
            jax.ShapeDtypeStruct((CHAINS, rows, BD), f32),
            jax.ShapeDtypeStruct((CHAINS, BD, BD), f32),
            jax.ShapeDtypeStruct((CHAINS, BD, BD), f32),
        ),
        in_specs=[pl.BlockSpec(memory_space=pl.ANY)],
        out_specs=(vmem, vmem, vmem),
        scratch_shapes=[
            pltpu.VMEM((chips, CHAINS, rows, BD), f32),
            pltpu.VMEM((chips, CHAINS, rows, BD), f32),
            pltpu.VMEM((max(1, chips - 1), CHAINS, rows, BD), jnp.bfloat16),
            pltpu.VMEM((max(1, chips - 1), CHAINS, rows, BD), jnp.bfloat16),
            pltpu.VMEM((CHAINS, BD, BD), f32),
            pltpu.VMEM((CHAINS, BD, BD), f32),
            pltpu.VMEM((rows, BD), f32),
            dma((chips, CHAINS)),
            dma((chips, CHAINS)),
            dma((chips, CHAINS)),
            dma((max(1, chips - 1), CHAINS)),
            dma((max(1, chips - 1), CHAINS)),
            dma((CHAINS,)),
            dma((CHAINS,)),
        ],
        compiler_params=pltpu.CompilerParams(
            collective_id=0, has_side_effects=True, vmem_limit_bytes=48 * 2**20
        ),
        name="sweep",
    )(partial)


def eliminate(full, inverse):
    for first in range(0, PANEL, WIDTH):
        spread = [
            {
                j: jnp.broadcast_to(full[first + i][:, j:j + 1], full[0].shape)
                for j in range(first + i, PANEL)
            }
            for i in range(WIDTH)
        ]
        for i in range(WIDTH):
            row = first + i
            scale = lax.rsqrt(spread[i][row])
            full[row] = full[row] * scale
            inverse[row] = inverse[row] * scale
            for j in range(row + 1, PANEL):
                spread[i][j] = spread[i][j] * scale
            for later in range(i + 1, WIDTH):
                factor = spread[i][first + later]
                for j in range(first + later, PANEL):
                    spread[later][j] = spread[later][j] - factor * spread[i][j]
                full[first + later] = full[first + later] - factor * full[row]
                inverse[first + later] = inverse[first + later] - factor * inverse[row]
        for j in range(first + WIDTH, PANEL):
            for i in range(WIDTH):
                full[j] = full[j] - spread[i][j] * full[first + i]
                inverse[j] = inverse[j] - spread[i][j] * inverse[first + i]


def canonical_kernel(merged, x_in, g_in, top, bottom, upper, inverse):
    count = 2 * CHAINS
    eye = identity()
    for b in range(count):
        rows = pl.ds(b, BD, stride=count)
        upper[rows, :] = g_in[b] if b < CHAINS else x_in[b - CHAINS]
        inverse[rows, :] = eye

    @pl.loop(0, BD // PANEL)
    def _(panel):
        for known in range(1, BD // PANEL):
            @pl.when(panel == known)
            def _():
                lanes = slice(known * PANEL, (known + 1) * PANEL)
                for b in range(count):
                    done = pl.ds(b, known * PANEL, stride=count)
                    here = pl.ds(known * PANEL * count + b, PANEL, stride=count)
                    rows = upper[done, :]
                    upper[here, :] -= mm_tn(rows[:, lanes], rows)
                    if b < CHAINS:
                        inverse[here, :] -= mm_tn(rows[:, lanes], inverse[done, :])

        start = panel * PANEL * count
        where = lambda i: pl.ds(pl.multiple_of(start + i * count, count), count)
        ahead = lax.rem(BD - panel * PANEL, BD)
        full = [pltpu.roll(upper[where(i), :], ahead, 1) for i in range(PANEL)]
        inv = [inverse[where(i), :] for i in range(PANEL)]
        eliminate(full, inv)
        for i in range(PANEL):
            upper[where(i), :] = pltpu.roll(full[i], panel * PANEL, 1)
            inverse[where(i), :] = inv[i]

    lanes = lax.broadcasted_iota(jnp.int32, (BD, BD), 1)
    triangle = lanes >= lax.broadcasted_iota(jnp.int32, (BD, BD), 0)
    for k in range(CHAINS):
        lower_inv = inverse[pl.ds(k, BD, stride=count), :]
        carried = upper[pl.ds(CHAINS + k, BD, stride=count), :]
        carried = jnp.where(triangle, carried, 0.0)
        out = bottom if k % 2 else top
        for p in range(PH):
            part = mm_nt(lower_inv, merged[k, pl.ds(p * BD, BD), :])
            out[0, k // 2, :, pl.ds(p * BD, BD)] = mm_nt(part, carried)


def canonical(merged, x, gram):
    vmem = pl.BlockSpec(memory_space=pltpu.VMEM)
    out = jax.ShapeDtypeStruct((1, SEC_DEV, BD, PH * BD), jnp.float32)
    return pl.pallas_call(
        canonical_kernel,
        out_shape=(out, out),
        in_specs=[vmem, vmem, vmem],
        out_specs=(vmem, vmem),
        scratch_shapes=[
            pltpu.VMEM((2 * CHAINS * BD, BD), jnp.float32),
            pltpu.VMEM((2 * CHAINS * BD, BD), jnp.float32),
        ],
        compiler_params=pltpu.CompilerParams(vmem_limit_bytes=32 * 2**20),
        name="canonical",
    )(merged, x, gram)


def local(top_blocks, bottom_blocks, row_tensor, merge_owner, merge_sub):
    owners = lax.axis_size("sector")
    sites = lax.axis_size("site")
    sectors = owners * SEC_DEV
    target = merge_owner[0, :, 0] * SEC_DEV + merge_sub[0]
    partial = absorb(target, top_blocks, bottom_blocks, row_tensor, sectors)
    partial = partial.reshape(owners, CHAINS, PH * BD, BD)
    return canonical(*sweep(partial, sites, owners))


def solution(mesh):
    placed = (
        P("site", "sector", None, None),
        P("site", "sector", None, None),
        P("site", "sector", None, None),
        P("site", "sector", None),
        P("site", "sector"),
    )
    return jax.shard_map(
        local,
        mesh=mesh,
        in_specs=placed,
        out_specs=(P("site", "sector", None, None), P("site", "sector", None, None)),
        check_vma=False,
    )
```

time: 609 us -> 71.1 us (0.12)
  the two profiles are of different devices: /device:TPU:0 before, /device:TPU:28 now
where the time goes in v1:
time: 71.1 us; the launch traced here: 70.8 us
  Pallas kernels  68.3 us (96%)
  local copies, waits for them, and re-layouts  1.22 us (2%)
    pallas_call x1, Pallas kernels, sweep(): pl.pallas_call(functools.partial(sweep_kernel, sites, owners), out_shape=...  47.5 us
    pallas_call x1, Pallas kernels, canonical(): pl.pallas_call(canonical_kernel, out_shape=(out, out), in_specs=[vmem, vm...  12.6 us
    pallas_call x1, Pallas kernels, absorb(): pl.pallas_call(absorb_kernel, out_shape=jax.ShapeDtypeStruct((sectors, 2,...  8.1 us

profile of v1, /device:TPU:28, one launch (start us, length us, event | category | flops | bytes accessed | tf_op | source)
XLA Modules:
  0.0 70.8 jit_solution(12119375639858589869)
XLA Ops:
  0.6 0.7 bitcast_add_fusion.target
  1.3 0.0 copy-start
  1.3 1.2 %copy-done = bf16[1,8,512,128]{3,2,1,0:T(8,128)(2,1)S(1)} copy-done((bf16[1,8,512,128]{3,2,1,0:T(8,128)(2,1)S(1)}, bf16[1,8,512,128]{3,2,1,0:T(8,128)(2,1)}, u32[]{:S(2)}) %copy-start) | copy-done | bytes 1048600
  2.5 8.1 %absorb.1 = f32[8,2,512,128]{3,2,1,0:T(8,128)S(1)} custom-call(s32[8]{0:T(128)S(1)} %bitcast_add_fusion.target, bf16[1,8,512,512]{3,2,1,0:T(8,128)(2,1)} %top.1, bf16[1,8,512,512]{3,2,1,0:T(8,128)(2,1)} %bottom.1, bf16[1,8,512,128]{3,2,1,0:T(8,128)(2,1)S(1)} %copy-done), custom_call_target="tpu_custom_call" | custom-call | tf_op jit(solution)/shard_map/absorb/pallas_call | solution.py:50
  10.6 47.5 %sweep.1 = (f32[4,512,128]{2,1,0:T(8,128)S(1)}, f32[4,128,128]{2,1,0:T(8,128)S(1)}, f32[4,128,128]{2,1,0:T(8,128)S(1)}) custom-call(f32[4,4,512,128]{3,2,1,0:T(8,128)S(1)} %bitcast.5), custom_call_target="tpu_custom_call" | custom-call | tf_op jit(solution)/shard_map/sweep/pallas_call | solution.py:206
  58.2 12.6 %canonical.1 = (f32[1,2,128,512]{3,2,1,0:T(8,128)}, f32[1,2,128,512]{3,2,1,0:T(8,128)}) custom-call(f32[4,512,128]{2,1,0:T(8,128)S(1)} %get-tuple-element.5.merged, f32[4,128,128]{2,1,0:T(8,128)S(1)} %get-tuple-element.6.x_in, f32[4,128,128]{2,1,0:T(8,128)S(1)} %get-tuple-element.7.g_in), custom_call_target="tpu_custom_call" | custom-call | tf_op jit(solution)/shard_map/canonical/pallas_call | solution.py:313
Async XLA Ops:
  1.3 1.2 %copy-start = (bf16[1,8,512,128]{3,2,1,0:T(8,128)(2,1)S(1)}, bf16[1,8,512,128]{3,2,1,0:T(8,128)(2,1)}, u32[]{:S(2)}) copy-start(bf16[1,8,512,128]{3,2,1,0:T(8,128)(2,1)} %weights.1) | copy-start | bytes 3145732

commit v2 on v1

--- a/solution.py
+++ b/solution.py
@@ -13,52 +13,52 @@
 CHAINS = 4
 PANEL = 32
 WIDTH = 4
-HIGHEST = lax.Precision.HIGHEST
-NT = (((1,), (1,)), ((), ()))
-
-
-def mm(a, b):
-    return jnp.dot(a, b, precision=HIGHEST, preferred_element_type=jnp.float32)
-
-
-def mm_nt(a, b):
-    return lax.dot_general(a, b, NT, precision=HIGHEST, preferred_element_type=jnp.float32)
-
-
-def mm_tn(a, b):
-    return lax.dot_general(
-        a, b, (((0,), (0,)), ((), ())), precision=HIGHEST, preferred_element_type=jnp.float32
-    )
-
-
-def absorb_kernel(target, top, bottom, weights, partial):
+
+
+def absorb_kernel(owner, member, top, bottom, weights, partial):
     step = pl.program_id(0)
 
     @pl.when(step == 0)
     def _():
         partial[...] = jnp.zeros_like(partial)
 
-    sector = target[step]
+    sector = owner[0, step, 0] * SEC_DEV + member[0, step]
     for boundary, blocks in enumerate((top, bottom)):
         absorbed = jnp.dot(blocks[0, 0], weights[0, 0], preferred_element_type=jnp.float32)
         partial[sector, boundary] += absorbed.astype(jnp.bfloat16).astype(jnp.float32)
 
 
-def absorb(target, top_blocks, bottom_blocks, row_tensor, sectors):
+def absorb(top_blocks, bottom_blocks, row_tensor, merge_owner, merge_sub, sectors):
     count, rows, inner = top_blocks.shape[1:]
-    block = lambda *tail: pl.BlockSpec((1, 1) + tail, lambda j, t: (0, j, 0, 0))
+    block = lambda *tail: pl.BlockSpec((1, 1) + tail, lambda j: (0, j, 0, 0))
+    smem = pl.BlockSpec(memory_space=pltpu.SMEM)
     return pl.pallas_call(
         absorb_kernel,
         out_shape=jax.ShapeDtypeStruct((sectors, 2, rows, BD), jnp.float32),
-        grid_spec=pltpu.PrefetchScalarGridSpec(
-            num_scalar_prefetch=1,
-            grid=(count,),
-            in_specs=[block(rows, inner), block(rows, inner), block(inner, BD)],
-            out_specs=pl.BlockSpec((sectors, 2, rows, BD), lambda j, t: (0, 0, 0, 0)),
-        ),
+        grid=(count,),
+        in_specs=[smem, smem, block(rows, inner), block(rows, inner), block(inner, BD)],
+        out_specs=pl.BlockSpec((sectors, 2, rows, BD), lambda j: (0, 0, 0, 0)),
         compiler_params=pltpu.CompilerParams(vmem_limit_bytes=48 * 2**20),
         name="absorb",
-    )(target, top_blocks, bottom_blocks, row_tensor)
+    )(merge_owner, merge_sub, top_blocks, bottom_blocks, row_tensor)
+
+
+def split(value):
+    high = value.astype(jnp.bfloat16)
+    return high, (value - high.astype(jnp.float32)).astype(jnp.bfloat16)
+
+
+def joined(axis, *parts):
+    return jnp.concatenate(parts, axis=axis)
+
+
+def dot3(a, b, a_axis, b_axis):
+    a_high, a_low = split(a)
+    b_high, b_low = split(b)
+    return lax.dot_general(
+        joined(a_axis, a_high, a_high, a_low), joined(b_axis, b_high, b_low, b_high),
+        (((a_axis,), (b_axis,)), ((), ())), preferred_element_type=jnp.float32,
+    )
 
 
 def identity():
@@ -69,7 +69,7 @@
 
 def sweep_kernel(
     sites, owners, partial, m_out, x_out, g_out,
-    own, near, away, landed, leaving, arriving, turned,
+    own, near, away, landed, leaving, arriving, turned, turned_cat, merged_cat,
     own_sem, near_send, near_recv, away_send, away_recv, site_send, site_recv,
 ):
     chips = owners // 2
@@ -163,6 +163,10 @@
                 merged += eye
             m_out[k, rows, :] = merged
             turned[rows, :] = merged.T
+            high, low = split(merged.T)
+            turned_cat[rows, :] = joined(1, high, high, low)
+            high, low = split(merged)
+            merged_cat[pl.ds(p * 3 * BD, 3 * BD), :] = joined(0, high, low, high)
 
         @pl.when(site == 0)
         def _():
@@ -173,16 +177,24 @@
             site_copy(k).wait_recv()
             x_out[k] = arriving[k]
 
-        half = mm(turned[...], x_out[k])
-        gram = mm(half[:BD], m_out[k, pl.ds(0, BD), :])
-        for p in range(1, PH):
-            gram += mm(half[p * BD:(p + 1) * BD], m_out[k, pl.ds(p * BD, BD), :])
+        high, low = split(x_out[k])
+        half = jnp.dot(
+            turned_cat[...], joined(0, high, low, high), preferred_element_type=jnp.float32
+        )
+        high, low = split(half)
+        cut = lambda part, p: part[p * BD:(p + 1) * BD]
+        grams = []
+        for p in range(PH):
+            h, l = cut(high, p), cut(low, p)
+            grams += [h, h, l]
+        gram = jnp.dot(joined(1, *grams), merged_cat[...], preferred_element_type=jnp.float32)
+        trace = jnp.sum(jnp.sum(half * turned[...], axis=0, keepdims=True), axis=1, keepdims=True)
+        scale = 1.0 / (trace * (1.0 / (BD * BD)) + 1e-06)
         g_out[k] = gram
 
         @pl.when(site < sites - 1)
         def _():
-            trace = jnp.sum(jnp.sum(gram * eye, axis=0, keepdims=True), axis=1, keepdims=True)
-            leaving[k] = gram / (trace * (1.0 / (BD * BD)) + 1e-06)
+            leaving[k] = gram * scale
             site_copy(k).start()
 
     @pl.loop(0, CHAINS)
@@ -220,6 +232,8 @@
             pltpu.VMEM((CHAINS, BD, BD), f32),
             pltpu.VMEM((CHAINS, BD, BD), f32),
             pltpu.VMEM((rows, BD), f32),
+            pltpu.VMEM((rows, 3 * BD), jnp.bfloat16),
+            pltpu.VMEM((3 * rows, BD), jnp.bfloat16),
             dma((chips, CHAINS)),
             dma((chips, CHAINS)),
             dma((chips, CHAINS)),
@@ -281,9 +295,9 @@
                     done = pl.ds(b, known * PANEL, stride=count)
                     here = pl.ds(known * PANEL * count + b, PANEL, stride=count)
                     rows = upper[done, :]
-                    upper[here, :] -= mm_tn(rows[:, lanes], rows)
+                    upper[here, :] -= dot3(rows[:, lanes], rows, 0, 0)
                     if b < CHAINS:
-                        inverse[here, :] -= mm_tn(rows[:, lanes], inverse[done, :])
+                        inverse[here, :] -= dot3(rows[:, lanes], inverse[done, :], 0, 0)
 
         start = panel * PANEL * count
         where = lambda i: pl.ds(pl.multiple_of(start + i * count, count), count)
@@ -303,8 +317,8 @@
         carried = jnp.where(triangle, carried, 0.0)
         out = bottom if k % 2 else top
         for p in range(PH):
-            part = mm_nt(lower_inv, merged[k, pl.ds(p * BD, BD), :])
-            out[0, k // 2, :, pl.ds(p * BD, BD)] = mm_nt(part, carried)
+            part = dot3(lower_inv, merged[k, pl.ds(p * BD, BD), :], 1, 1)
+            out[0, k // 2, :, pl.ds(p * BD, BD)] = dot3(part, carried, 1, 1)
 
 
 def canonical(merged, x, gram):
@@ -328,8 +342,7 @@
     owners = lax.axis_size("sector")
     sites = lax.axis_size("site")
     sectors = owners * SEC_DEV
-    target = merge_owner[0, :, 0] * SEC_DEV + merge_sub[0]
-    partial = absorb(target, top_blocks, bottom_blocks, row_tensor, sectors)
+    partial = absorb(top_blocks, bottom_blocks, row_tensor, merge_owner, merge_sub, sectors)
     partial = partial.reshape(owners, CHAINS, PH * BD, BD)
     return canonical(*sweep(partial, sites, owners))
 

time: 71.1 us -> 64.6 us (0.909)
  Pallas kernels: 68.3 us -> 61.1 us
  local copies, waits for them, and re-layouts: 1.22 us -> 2.61 us
    pallas_call x1, Pallas kernels: 47.5 us -> 42.2 us  [sweep(): pl.pallas_call(functools.partial(sweep_kernel, sites, owners), out_shape=...]
    unnamed x2 -> x5, local copies, waits for them, and re-layouts: 1.22 us -> 2.61 us
    pallas_call x1, Pallas kernels: 12.6 us -> 11.3 us  [canonical(): pl.pallas_call(canonical_kernel, out_shape=(out, out), in_specs=[vmem, vm...]
where the time goes in v2:
time: 64.6 us; the launch traced here: 64.3 us
  Pallas kernels  61.1 us (95%)
  local copies, waits for them, and re-layouts  2.61 us (4%)
  between operations  0.65 us (1%)
    pallas_call x1, Pallas kernels, sweep(): pl.pallas_call(functools.partial(sweep_kernel, sites, owners), out_shape=...  42.2 us
    pallas_call x1, Pallas kernels, canonical(): pl.pallas_call(canonical_kernel, out_shape=(out, out), in_specs=[vmem, vm...  11.3 us
    pallas_call x1, Pallas kernels, absorb(): pl.pallas_call(absorb_kernel, out_shape=jax.ShapeDtypeStruct((sectors, 2,...  7.61 us
    unnamed x5, local copies, waits for them, and re-layouts  2.61 us

profile of v2, /device:TPU:28, one launch (start us, length us, event | category | flops | bytes accessed | tf_op | source)
XLA Modules:
  0.0 64.3 jit_solution(13856324733394664871)
XLA Ops:
  0.6 0.7 %copy.7.owner = s32[1,8,1]{2,1,0:T(8,128)S(1)} copy(s32[1,8,1]{1,2,0:T(1,128)} %param.8) | data formatting | bytes 64 | tf_op args[3]
  1.4 0.0 copy-start
  1.4 1.2 %copy-done = bf16[1,8,512,128]{3,2,1,0:T(8,128)(2,1)S(1)} copy-done((bf16[1,8,512,128]{3,2,1,0:T(8,128)(2,1)S(1)}, bf16[1,8,512,128]{3,2,1,0:T(8,128)(2,1)}, u32[]{:S(2)}) %copy-start) | copy-done | bytes 1048600
  2.6 0.0 copy-start.1
  2.6 0.7 %copy-done.1 = s32[1,8]{1,0:T(1,128)S(1)} copy-done((s32[1,8]{1,0:T(1,128)S(1)}, s32[1,8]{1,0:T(1,128)}, u32[]{:S(2)}) %copy-start.1) | copy-done | bytes 56
  3.2 7.6 %absorb.1 = f32[8,2,512,128]{3,2,1,0:T(8,128)S(1)} custom-call(s32[1,8,1]{2,1,0:T(8,128)S(1)} %copy.7.owner, s32[1,8]{1,0:T(1,128)S(1)} %copy-done.1, bf16[1,8,512,512]{3,2,1,0:T(8,128)(2,1)} %top.1, bf16[1,8,512,512]{3,2,1,0:T(8,128)(2,1)} %bottom.1, bf16[1,8,512,128]{3,2,1,0:T(8,128)(2,1)S(1)} %copy-done), custom_call_target="tpu_custom_call" | custom-call | tf_op jit(solution)/shard_map/absorb/pallas_call | solution.py:35
  10.9 42.2 %sweep.1 = (f32[4,512,128]{2,1,0:T(8,128)S(1)}, f32[4,128,128]{2,1,0:T(8,128)S(1)}, f32[4,128,128]{2,1,0:T(8,128)S(1)}) custom-call(f32[4,4,512,128]{3,2,1,0:T(8,128)S(1)} %bitcast.1), custom_call_target="tpu_custom_call" | custom-call | tf_op jit(solution)/shard_map/sweep/pallas_call | solution.py:218
  53.1 11.3 %canonical.1 = (f32[1,2,128,512]{3,2,1,0:T(8,128)}, f32[1,2,128,512]{3,2,1,0:T(8,128)}) custom-call(f32[4,512,128]{2,1,0:T(8,128)S(1)} %get-tuple-element.5.merged, f32[4,128,128]{2,1,0:T(8,128)S(1)} %get-tuple-element.6.x_in, f32[4,128,128]{2,1,0:T(8,128)S(1)} %get-tuple-element.7.g_in), custom_call_target="tpu_custom_call" | custom-call | tf_op jit(solution)/shard_map/canonical/pallas_call | solution.py:327
Async XLA Ops:
  1.4 1.2 %copy-start = (bf16[1,8,512,128]{3,2,1,0:T(8,128)(2,1)S(1)}, bf16[1,8,512,128]{3,2,1,0:T(8,128)(2,1)}, u32[]{:S(2)}) copy-start(bf16[1,8,512,128]{3,2,1,0:T(8,128)(2,1)} %weights.1) | copy-start | bytes 3145732
  2.6 0.7 %copy-start.1 = (s32[1,8]{1,0:T(1,128)S(1)}, s32[1,8]{1,0:T(1,128)}, u32[]{:S(2)}) copy-start(s32[1,8]{1,0:T(1,128)} %member.1) | copy-start | bytes 100

commit v3 on v2

--- a/solution.py
+++ b/solution.py
@@ -13,34 +13,6 @@
 CHAINS = 4
 PANEL = 32
 WIDTH = 4
-
-
-def absorb_kernel(owner, member, top, bottom, weights, partial):
-    step = pl.program_id(0)
-
-    @pl.when(step == 0)
-    def _():
-        partial[...] = jnp.zeros_like(partial)
-
-    sector = owner[0, step, 0] * SEC_DEV + member[0, step]
-    for boundary, blocks in enumerate((top, bottom)):
-        absorbed = jnp.dot(blocks[0, 0], weights[0, 0], preferred_element_type=jnp.float32)
-        partial[sector, boundary] += absorbed.astype(jnp.bfloat16).astype(jnp.float32)
-
-
-def absorb(top_blocks, bottom_blocks, row_tensor, merge_owner, merge_sub, sectors):
-    count, rows, inner = top_blocks.shape[1:]
-    block = lambda *tail: pl.BlockSpec((1, 1) + tail, lambda j: (0, j, 0, 0))
-    smem = pl.BlockSpec(memory_space=pltpu.SMEM)
-    return pl.pallas_call(
-        absorb_kernel,
-        out_shape=jax.ShapeDtypeStruct((sectors, 2, rows, BD), jnp.float32),
-        grid=(count,),
-        in_specs=[smem, smem, block(rows, inner), block(rows, inner), block(inner, BD)],
-        out_specs=pl.BlockSpec((sectors, 2, rows, BD), lambda j: (0, 0, 0, 0)),
-        compiler_params=pltpu.CompilerParams(vmem_limit_bytes=48 * 2**20),
-        name="absorb",
-    )(merge_owner, merge_sub, top_blocks, bottom_blocks, row_tensor)
 
 
 def split(value):
@@ -68,10 +40,13 @@
 
 
 def sweep_kernel(
-    sites, owners, partial, m_out, x_out, g_out,
-    own, near, away, landed, leaving, arriving, turned, turned_cat, merged_cat,
-    own_sem, near_send, near_recv, away_send, away_recv, site_send, site_recv,
+    sites, owners, masks_in, tops_in, bottoms_in, weights_in, m_out, x_out, g_out,
+    masks, blocks, weights, absorbed, own, leave_near, near, away, landed,
+    leaving, arriving, turned, turned_cat, merged_cat,
+    mask_sem, block_sem, weight_sem,
+    near_send, near_recv, away_send, away_recv, site_send, site_recv,
 ):
+    count = weights.shape[0]
     chips = owners // 2
     site = lax.axis_index("site")
     sector = lax.axis_index("sector")
@@ -86,6 +61,27 @@
     def mate(shift):
         return at(site, ((chip + shift) % chips) * 2 + core)
 
+    mask_load = pltpu.make_async_copy(masks_in, masks, mask_sem)
+    mask_load.start()
+
+    def block_load(boundary, j):
+        source = bottoms_in if boundary else tops_in
+        return pltpu.make_async_copy(
+            source.at[0, j], blocks.at[boundary, j], block_sem.at[boundary, j]
+        )
+
+    def weight_load(j):
+        return pltpu.make_async_copy(weights_in.at[0, j], weights.at[j], weight_sem.at[j])
+
+    @pl.loop(0, count)
+    def _(j):
+        weight_load(j).start()
+        block_load(0, j).start()
+
+    @pl.loop(0, count)
+    def _(j):
+        block_load(1, j).start()
+
     barrier = pltpu.get_barrier_semaphore()
     for device in [partner] + [mate(shift) for shift in range(1, chips)]:
         pl.semaphore_signal(barrier, inc=1, device_id=device, device_id_type=pl.DeviceIdType.MESH)
@@ -103,16 +99,9 @@
         )
 
     sides = jnp.where(site > 0, 1, 0) + jnp.where(site < sites - 1, 1, 0)
-    pl.semaphore_wait(barrier, chips + sides)
-
-    def own_copy(shift, k):
-        owner = ((chip + shift) % chips) * 2 + core
-        return pltpu.make_async_copy(partial.at[owner, k], own.at[shift, k], own_sem.at[shift, k])
-
     def near_copy(shift, k):
-        owner = ((chip + shift) % chips) * 2 + (1 - core)
         return pltpu.make_async_remote_copy(
-            src_ref=partial.at[owner, k], dst_ref=near.at[shift, k],
+            src_ref=leave_near.at[shift, k], dst_ref=near.at[shift, k],
             send_sem=near_send.at[shift, k], recv_sem=near_recv.at[shift, k],
             device_id=partner, device_id_type=pl.DeviceIdType.MESH,
         )
@@ -131,32 +120,65 @@
             device_id=at(site + 1, sector), device_id_type=pl.DeviceIdType.MESH,
         )
 
+    def combine(boundary, shift, core_to, out):
+        owner = ((chip + shift) % chips) * 2 + core_to
+        picks = [
+            [masks[owner * SEC_DEV + sub, j] for j in range(count)] for sub in range(SEC_DEV)
+        ]
+
+        @pl.loop(0, PH * BD // 16, unroll=2)
+        def _(tile):
+            rows = pl.ds(pl.multiple_of(tile * 16, 16), 16)
+            parts = [absorbed[j, rows, :].astype(jnp.float32) for j in range(count)]
+            for sub in range(SEC_DEV):
+                sums = []
+                for half in (slice(0, 8), slice(8, 16)):
+                    terms = [picks[sub][j] * parts[j][half] for j in range(count)]
+                    while len(terms) > 1:
+                        terms = [sum(terms[i:i + 2]) for i in range(0, len(terms), 2)]
+                    sums.append(terms[0])
+                total = jnp.concatenate(sums, axis=0)
+                out[shift, boundary * SEC_DEV + sub, rows, :] = total.astype(out.dtype)
+
     order = list(range(1, chips)) + [0]
-    for shift in order:
-        @pl.loop(0, CHAINS)
-        def _(k):
-            near_copy(shift, k).start()
-            own_copy(shift, k).start()
-
-    @pl.loop(0, CHAINS)
-    def _(k):
-        for shift in range(1, chips):
-            near_copy(shift, k).wait_recv()
-            own_copy(shift, k).wait()
-            away[shift - 1, k] = (near[shift, k] + own[shift, k]).astype(jnp.bfloat16)
-            away_copy(shift, k).start()
+    for boundary in range(2):
+        @pl.loop(0, count)
+        def _(j):
+            if boundary == 0:
+                weight_load(j).wait()
+            block_load(boundary, j).wait()
+            absorbed[j] = jnp.dot(
+                blocks[boundary, j], weights[j], preferred_element_type=jnp.float32
+            ).astype(jnp.bfloat16)
+
+        if boundary == 0:
+            mask_load.wait()
+            pl.semaphore_wait(barrier, chips + sides)
+        for shift in order:
+            combine(boundary, shift, 1 - core, leave_near)
+            for sub in range(SEC_DEV):
+                near_copy(shift, boundary * SEC_DEV + sub).start()
+        for shift in order:
+            combine(boundary, shift, core, own)
+            if shift:
+                for sub in range(SEC_DEV):
+                    k = boundary * SEC_DEV + sub
+                    near_copy(shift, k).wait_recv()
+                    away[shift - 1, k] = (
+                        near[shift, k].astype(jnp.float32) + own[shift, k]
+                    ).astype(jnp.bfloat16)
+                    away_copy(shift, k).start()
 
     eye = identity()
 
     @pl.loop(0, CHAINS)
     def _(k):
         near_copy(0, k).wait_recv()
-        own_copy(0, k).wait()
         for shift in range(1, chips):
             away_copy(shift, k).wait_recv()
         for p in range(PH):
             rows = pl.ds(p * BD, BD)
-            merged = near[0, k, rows, :] + own[0, k, rows, :]
+            merged = near[0, k, rows, :].astype(jnp.float32) + own[0, k, rows, :]
             for shift in range(1, chips):
                 merged += landed[shift - 1, k, rows, :].astype(jnp.float32)
             if p == 0:
@@ -209,8 +231,9 @@
             site_copy(k).wait_send()
 
 
-def sweep(partial, sites, owners):
+def sweep(masks, top_blocks, bottom_blocks, row_tensor, sites, owners):
     chips = owners // 2
+    count, _, inner = top_blocks.shape[1:]
     rows = PH * BD
     vmem = pl.BlockSpec(memory_space=pltpu.VMEM)
     f32 = jnp.float32
@@ -222,11 +245,16 @@
             jax.ShapeDtypeStruct((CHAINS, BD, BD), f32),
             jax.ShapeDtypeStruct((CHAINS, BD, BD), f32),
         ),
-        in_specs=[pl.BlockSpec(memory_space=pl.ANY)],
+        in_specs=[pl.BlockSpec(memory_space=pl.ANY)] * 4,
         out_specs=(vmem, vmem, vmem),
         scratch_shapes=[
+            pltpu.VMEM(masks.shape, f32),
+            pltpu.VMEM((2, count, rows, inner), jnp.bfloat16),
+            pltpu.VMEM((count, inner, BD), jnp.bfloat16),
+            pltpu.VMEM((count, rows, BD), jnp.bfloat16),
             pltpu.VMEM((chips, CHAINS, rows, BD), f32),
-            pltpu.VMEM((chips, CHAINS, rows, BD), f32),
+            pltpu.VMEM((chips, CHAINS, rows, BD), jnp.bfloat16),
+            pltpu.VMEM((chips, CHAINS, rows, BD), jnp.bfloat16),
             pltpu.VMEM((max(1, chips - 1), CHAINS, rows, BD), jnp.bfloat16),
             pltpu.VMEM((max(1, chips - 1), CHAINS, rows, BD), jnp.bfloat16),
             pltpu.VMEM((CHAINS, BD, BD), f32),
@@ -234,7 +262,9 @@
             pltpu.VMEM((rows, BD), f32),
             pltpu.VMEM((rows, 3 * BD), jnp.bfloat16),
             pltpu.VMEM((3 * rows, BD), jnp.bfloat16),
-            dma((chips, CHAINS)),
+            dma(()),
+            dma((2, count)),
+            dma((count,)),
             dma((chips, CHAINS)),
             dma((chips, CHAINS)),
             dma((max(1, chips - 1), CHAINS)),
@@ -246,7 +276,7 @@
             collective_id=0, has_side_effects=True, vmem_limit_bytes=48 * 2**20
         ),
         name="sweep",
-    )(partial)
+    )(masks, top_blocks, bottom_blocks, row_tensor)
 
 
 def eliminate(full, inverse):
@@ -315,10 +345,10 @@
         lower_inv = inverse[pl.ds(k, BD, stride=count), :]
         carried = upper[pl.ds(CHAINS + k, BD, stride=count), :]
         carried = jnp.where(triangle, carried, 0.0)
-        out = bottom if k % 2 else top
+        out = bottom if k // SEC_DEV else top
         for p in range(PH):
             part = dot3(lower_inv, merged[k, pl.ds(p * BD, BD), :], 1, 1)
-            out[0, k // 2, :, pl.ds(p * BD, BD)] = dot3(part, carried, 1, 1)
+            out[0, k % SEC_DEV, :, pl.ds(p * BD, BD)] = dot3(part, carried, 1, 1)
 
 
 def canonical(merged, x, gram):
@@ -342,9 +372,10 @@
     owners = lax.axis_size("sector")
     sites = lax.axis_size("site")
     sectors = owners * SEC_DEV
-    partial = absorb(top_blocks, bottom_blocks, row_tensor, merge_owner, merge_sub, sectors)
-    partial = partial.reshape(owners, CHAINS, PH * BD, BD)
-    return canonical(*sweep(partial, sites, owners))
+    target = merge_owner[0, :, 0] * SEC_DEV + merge_sub[0]
+    masks = (jnp.arange(sectors, dtype=jnp.int32)[:, None] == target[None, :]).astype(jnp.float32)
+    masks = jnp.broadcast_to(masks[:, :, None, None], masks.shape + (8, BD))
+    return canonical(*sweep(masks, top_blocks, bottom_blocks, row_tensor, sites, owners))
 
 
 def solution(mesh):

time: 64.6 us -> 59.5 us (0.921)
  Pallas kernels: 61.1 us -> 56.7 us
  local copies, waits for them, and re-layouts: 2.61 us -> 1.35 us
  other arithmetic: 0 us -> 0.68 us
    pallas_call x1 -> x0, Pallas kernels: 7.61 us -> none  [absorb(): pl.pallas_call(absorb_kernel, out_shape=jax.ShapeDtypeStruct((sectors, 2,...]
    pallas_call x1, Pallas kernels: 42.2 us -> 45.4 us  [sweep(): pl.pallas_call(functools.partial(sweep_kernel, sites, owners), out_shape=...]
    unnamed x5 -> x2, local copies, waits for them, and re-layouts: 2.61 us -> 1.22 us
    eq x0 -> x1, other arithmetic: none -> 0.68 us  [local(): jnp.arange(sectors, dtype=jnp.int32)[:, None] == target[None, :]]
where the time goes in v3:
time: 59.5 us; the launch traced here: 59.4 us
  Pallas kernels  56.7 us (95%)
  local copies, waits for them, and re-layouts  1.35 us (2%)
  other arithmetic  0.68 us (1%)
  between operations  0.66 us (1%)
    pallas_call x1, Pallas kernels, sweep(): pl.pallas_call(functools.partial(sweep_kernel, sites, owners), out_shape=...  45.4 us
    pallas_call x1, Pallas kernels, canonical(): pl.pallas_call(canonical_kernel, out_shape=(out, out), in_specs=[vmem, vm...  11.3 us
    unnamed x2, local copies, waits for them, and re-layouts  1.22 us

profile of v3, /device:TPU:28, one launch (start us, length us, event | category | flops | bytes accessed | tf_op | source)
XLA Modules:
  0.0 59.4 jit_solution(15361735220870707738)
XLA Ops:
  0.6 0.7 %fusion.1 = s32[8]{0:T(128)S(1)} fusion(s32[1,8]{1,0:T(1,128)} %param.9, s32[1,8,1]{1,2,0:T(1,128)} %param.8), kind=kLoop, calls=%fused_computation.3 | loop fusion | flops 16 | bytes 96 | tf_op jit(solution)/shard_map/eq | solution.py:376
  1.3 0.1 broadcast_in_dim.2.masks_in
  1.4 0.0 copy-start
  1.5 1.2 %copy-done = bf16[1,8,512,128]{3,2,1,0:T(8,128)(2,1)S(1)} copy-done((bf16[1,8,512,128]{3,2,1,0:T(8,128)(2,1)S(1)}, bf16[1,8,512,128]{3,2,1,0:T(8,128)(2,1)}, u32[]{:S(2)}) %copy-start) | copy-done | bytes 1048600
  2.7 45.4 %sweep.1 = (f32[4,512,128]{2,1,0:T(8,128)S(1)}, f32[4,128,128]{2,1,0:T(8,128)S(1)}, f32[4,128,128]{2,1,0:T(8,128)S(1)}) custom-call(f32[8,8,8,128]{3,2,1,0:T(8,128)S(1)} %broadcast_in_dim.2.masks_in, bf16[1,8,512,512]{3,2,1,0:T(8,128)(2,1)} %tops_in.1, bf16[1,8,512,512]{3,2,1,0:T(8,128)(2,1)} %bottoms_in.1, bf16[1,8,512,128]{3,2,1,0:T(8,128)(2,1)S(1)} %copy-done), custom_call_target="tpu_custom_call" | custom-call | tf_op jit(solution)/shard_map/sweep/pallas_call | solution.py:241
  48.1 11.3 %canonical.1 = (f32[1,2,128,512]{3,2,1,0:T(8,128)}, f32[1,2,128,512]{3,2,1,0:T(8,128)}) custom-call(f32[4,512,128]{2,1,0:T(8,128)S(1)} %get-tuple-element.5.merged, f32[4,128,128]{2,1,0:T(8,128)S(1)} %get-tuple-element.6.x_in, f32[4,128,128]{2,1,0:T(8,128)S(1)} %get-tuple-element.7.g_in), custom_call_target="tpu_custom_call" | custom-call | tf_op jit(solution)/shard_map/canonical/pallas_call | solution.py:357
  (1 shorter events, 0.0 us)
Async XLA Ops:
  1.4 1.2 %copy-start = (bf16[1,8,512,128]{3,2,1,0:T(8,128)(2,1)S(1)}, bf16[1,8,512,128]{3,2,1,0:T(8,128)(2,1)}, u32[]{:S(2)}) copy-start(bf16[1,8,512,128]{3,2,1,0:T(8,128)(2,1)} %weights_in.1) | copy-start | bytes 3145732

commit v4 on v3

--- a/solution.py
+++ b/solution.py
@@ -158,7 +158,6 @@
             combine(boundary, shift, 1 - core, leave_near)
             for sub in range(SEC_DEV):
                 near_copy(shift, boundary * SEC_DEV + sub).start()
-        for shift in order:
             combine(boundary, shift, core, own)
             if shift:
                 for sub in range(SEC_DEV):
@@ -245,7 +244,7 @@
             jax.ShapeDtypeStruct((CHAINS, BD, BD), f32),
             jax.ShapeDtypeStruct((CHAINS, BD, BD), f32),
         ),
-        in_specs=[pl.BlockSpec(memory_space=pl.ANY)] * 4,
+        in_specs=[pl.BlockSpec(memory_space=pl.ANY)] + [pl.BlockSpec(memory_space=pltpu.HBM)] * 3,
         out_specs=(vmem, vmem, vmem),
         scratch_shapes=[
             pltpu.VMEM(masks.shape, f32),
@@ -346,9 +345,11 @@
         carried = upper[pl.ds(CHAINS + k, BD, stride=count), :]
         carried = jnp.where(triangle, carried, 0.0)
         out = bottom if k // SEC_DEV else top
+        part = dot3(lower_inv, merged[k], 1, 1)
+        part = joined(0, *[part[:, p * BD:(p + 1) * BD] for p in range(PH)])
+        part = dot3(part, carried, 1, 1)
         for p in range(PH):
-            part = dot3(lower_inv, merged[k, pl.ds(p * BD, BD), :], 1, 1)
-            out[0, k % SEC_DEV, :, pl.ds(p * BD, BD)] = dot3(part, carried, 1, 1)
+            out[0, k % SEC_DEV, :, pl.ds(p * BD, BD)] = part[p * BD:(p + 1) * BD]
 
 
 def canonical(merged, x, gram):

time: 59.5 us -> 58 us (0.975)
  Pallas kernels: 56.7 us -> 55.1 us
    pallas_call x1, Pallas kernels: 11.3 us -> 9.67 us  [canonical(): pl.pallas_call(canonical_kernel, out_shape=(out, out), in_specs=[vmem, vm...]
where the time goes in v4:
time: 58 us; the launch traced here: 57.8 us
  Pallas kernels  55.1 us (95%)
  local copies, waits for them, and re-layouts  1.35 us (2%)
  other arithmetic  0.68 us (1%)
  between operations  0.66 us (1%)
    pallas_call x1, Pallas kernels, sweep(): pl.pallas_call(functools.partial(sweep_kernel, sites, owners), out_shape=...  45.4 us
    pallas_call x1, Pallas kernels, canonical(): pl.pallas_call(canonical_kernel, out_shape=(out, out), in_specs=[vmem, vm...  9.67 us
    unnamed x2, local copies, waits for them, and re-layouts  1.22 us

profile of v4, /device:TPU:28, one launch (start us, length us, event | category | flops | bytes accessed | tf_op | source)
XLA Modules:
  0.0 57.8 jit_solution(2550332881667554548)
XLA Ops:
  0.6 0.7 %fusion.1 = s32[8]{0:T(128)S(1)} fusion(s32[1,8]{1,0:T(1,128)} %param.9, s32[1,8,1]{1,2,0:T(1,128)} %param.8), kind=kLoop, calls=%fused_computation.3 | loop fusion | flops 16 | bytes 96 | tf_op jit(solution)/shard_map/eq | solution.py:377
  1.3 0.1 broadcast_in_dim.2.masks_in
  1.4 0.0 copy-start
  1.5 1.2 %copy-done = bf16[1,8,512,128]{3,2,1,0:T(8,128)(2,1)S(1)} copy-done((bf16[1,8,512,128]{3,2,1,0:T(8,128)(2,1)S(1)}, bf16[1,8,512,128]{3,2,1,0:T(8,128)(2,1)}, u32[]{:S(2)}) %copy-start) | copy-done | bytes 1048600
  2.7 45.4 %sweep.1 = (f32[4,512,128]{2,1,0:T(8,128)S(1)}, f32[4,128,128]{2,1,0:T(8,128)S(1)}, f32[4,128,128]{2,1,0:T(8,128)S(1)}) custom-call(f32[8,8,8,128]{3,2,1,0:T(8,128)S(1)} %broadcast_in_dim.2.masks_in, bf16[1,8,512,512]{3,2,1,0:T(8,128)(2,1)} %tops_in.1, bf16[1,8,512,512]{3,2,1,0:T(8,128)(2,1)} %bottoms_in.1, bf16[1,8,512,128]{3,2,1,0:T(8,128)(2,1)S(1)} %copy-done), custom_call_target="tpu_custom_call" | custom-call | tf_op jit(solution)/shard_map/sweep/pallas_call | solution.py:240
  48.1 9.7 %canonical.1 = (f32[1,2,128,512]{3,2,1,0:T(8,128)}, f32[1,2,128,512]{3,2,1,0:T(8,128)}) custom-call(f32[4,512,128]{2,1,0:T(8,128)S(1)} %get-tuple-element.5.merged, f32[4,128,128]{2,1,0:T(8,128)S(1)} %get-tuple-element.6.x_in, f32[4,128,128]{2,1,0:T(8,128)S(1)} %get-tuple-element.7.g_in), custom_call_target="tpu_custom_call" | custom-call | tf_op jit(solution)/shard_map/canonical/pallas_call | solution.py:358
  (1 shorter events, 0.0 us)
Async XLA Ops:
  1.4 1.2 %copy-start = (bf16[1,8,512,128]{3,2,1,0:T(8,128)(2,1)S(1)}, bf16[1,8,512,128]{3,2,1,0:T(8,128)(2,1)}, u32[]{:S(2)}) copy-start(bf16[1,8,512,128]{3,2,1,0:T(8,128)(2,1)} %weights_in.1) | copy-start | bytes 3145732
